TPU v7x, 512 devices: a whole 4x8x8 slice. The times are simulated.
512 devices in a mesh: rep: 8 (over y), fsdp: 64 (over z, x, core).
Axes of the slice: x: 4, y: 8, z: 8, core: 2. Of those that a mesh axis runs over, the one named last changes fastest.
Arguments:
- grad_partials: bfloat16 [8, 64, 64, 14336], P('rep', None, 'fsdp'), may hold values from -5 to 5
- stats_prev: float32 [8, 64, 1, 2, 512, 512], P('rep', 'fsdp'), may hold values from -10 to 5401, as said below
- owner_table: int32 [224], replicated, may hold values from 0 to 63, as said below
- newton_counts: int32 [224], replicated, may hold values from 2 to 3
Outputs:
- direction: bfloat16 [64, 64, 14336], P('rep', 'fsdp')
Inputs may be any that keep to these rules, and one draw needn't show every extreme that they name: `owner_table`: block b belongs to replica group b // 28; within a group no two blocks have the same value; a value v names the single slot of fsdp index v. `stats_prev`: each 512 x 512 matrix is symmetric positive definite.
All inputs are finite; a program needn't handle non-finite values.
Results may differ from a plain program's by a relative error of at most 0.019.
Values may be sent and summed in bfloat16 or wider, within the bound.
A program may use at most 64 MiB of HBM per device.

v0:
```python
import jax
import jax.numpy as jnp
from jax import lax
from jax.sharding import PartitionSpec as P

decay_rate = 0.9
highest = lax.Precision.HIGHEST


def inverse_root(statistic, iter_count):
    identity = jnp.eye(statistic.shape[0], dtype=jnp.float32)
    newton_m = statistic / jnp.sqrt(jnp.sum(statistic * statistic) + 1e-06)
    step_t = ((5.0 * identity - newton_m) * 0.25).astype(jnp.bfloat16)
    power_p = step_t.astype(jnp.float32)

    def advance(step_index, carried):
        newton_m, step_t, power_p = carried
        square_t = jnp.dot(step_t, step_t, preferred_element_type=jnp.float32).astype(jnp.bfloat16)
        fourth_t = jnp.dot(square_t, square_t, preferred_element_type=jnp.float32).astype(
            jnp.bfloat16
        )
        newton_m = jnp.dot(
            fourth_t, newton_m.astype(jnp.bfloat16), preferred_element_type=jnp.float32
        )
        step_t = ((5.0 * identity - newton_m) * 0.25).astype(jnp.bfloat16)
        power_p = jnp.dot(power_p.astype(jnp.bfloat16), step_t, preferred_element_type=jnp.float32)
        return (newton_m, step_t, power_p)

    carried = lax.fori_loop(0, iter_count - 1, advance, (newton_m, step_t, power_p))
    return carried[2].astype(jnp.bfloat16)


def root_batch(statistics, counts):

    def one_slot(packed_pair):
        return inverse_root(packed_pair[0], packed_pair[1])

    return lax.map(one_slot, (statistics, counts))


def pack_pieces(rows, block_of, filled, thin_rows, col_count, block_size, slot_count, fsdp_count):
    band_count = rows.shape[0] // thin_rows
    grid_view = rows.reshape(band_count, thin_rows, col_count, block_size)
    slot_block = block_of.reshape(fsdp_count, slot_count).T
    is_live = filled.reshape(fsdp_count, slot_count).T
    band_index = (slot_block // col_count)[:, None, :]
    col_index = (slot_block % col_count)[:, None, :]
    line_index = jnp.arange(thin_rows, dtype=jnp.int32)[None, :, None]
    picked = grid_view[band_index, line_index, col_index]
    return jnp.where(is_live[:, None, :, None], picked, jnp.zeros((), picked.dtype))


def batched_product(left_side, right_side):
    return lax.dot_general(left_side, right_side, (((2,), (1,)), ((0,), (0,))), precision=highest)


def body(grad_partials, stats_prev, owner_table, newton_counts):
    rep_count = lax.axis_size("rep")
    fsdp_count = lax.axis_size("fsdp")
    rep_index = lax.axis_index("rep")
    fsdp_index = lax.axis_index("fsdp")
    slot_count = stats_prev.shape[2]
    block_size = stats_prev.shape[-1]
    col_total = grad_partials.shape[3]
    rows_all = grad_partials.shape[1]
    thin_rows = block_size // fsdp_count
    col_count = col_total // block_size
    rows_group = rows_all // rep_count
    band_count = rows_group // thin_rows
    per_group = band_count * col_count
    places = fsdp_count * slot_count
    owner_slots = owner_table.reshape(rep_count, per_group)
    group_counts = newton_counts.reshape(rep_count, per_group)
    matches = owner_slots[:, None, :] == jnp.arange(places, dtype=jnp.int32)[None, :, None]
    filled = jnp.any(matches, axis=2)
    block_of = jnp.sum(
        jnp.where(matches, jnp.arange(per_group, dtype=jnp.int32)[None, None, :], 0), axis=2
    )
    partial_value = grad_partials[0, :, 0, :]
    shared_rows = lax.psum_scatter(
        partial_value.astype(jnp.float32).astype(jnp.bfloat16),
        "rep",
        scatter_dimension=0,
        tiled=True,
    ).astype(jnp.float32)
    outgoing = pack_pieces(
        shared_rows,
        block_of[rep_index],
        filled[rep_index],
        thin_rows,
        col_count,
        block_size,
        slot_count,
        fsdp_count,
    )
    owned_rows = lax.all_to_all(
        outgoing.astype(jnp.bfloat16), "fsdp", split_axis=2, concat_axis=2, tiled=True
    ).astype(outgoing.dtype)
    grad_blocks = owned_rows.reshape(slot_count, block_size, block_size)
    group_blocks = block_of[rep_index]
    group_filled = filled[rep_index]
    my_places = fsdp_index * slot_count + jnp.arange(slot_count, dtype=jnp.int32)
    my_counts = jnp.where(
        group_filled[my_places], group_counts[rep_index][group_blocks[my_places]], 1
    )
    previous = stats_prev[0, 0]
    left_stats = decay_rate * previous[:, 0] + lax.dot_general(
        grad_blocks, grad_blocks, (((2,), (2,)), ((0,), (0,))), precision=highest
    )
    right_stats = decay_rate * previous[:, 1] + lax.dot_general(
        grad_blocks, grad_blocks, (((1,), (1,)), ((0,), (0,))), precision=highest
    )
    left_roots = root_batch(left_stats, my_counts)
    right_roots = root_batch(right_stats, my_counts)
    halfway = batched_product(left_roots.astype(jnp.float32), grad_blocks)
    precond = batched_product(halfway, right_roots.astype(jnp.float32))
    grad_mass = jnp.sum(grad_blocks * grad_blocks, axis=(1, 2))
    pre_mass = jnp.sum(precond * precond, axis=(1, 2))
    scaled = (precond * jnp.sqrt(grad_mass / (pre_mass + 1e-06))[:, None, None]).astype(
        jnp.bfloat16
    )
    returned = lax.all_to_all(
        scaled.reshape(slot_count, thin_rows, fsdp_count, block_size),
        "fsdp",
        split_axis=2,
        concat_axis=2,
        tiled=True,
    )
    values = owner_slots[rep_index].reshape(band_count, 1, col_count)
    slot_index = values % slot_count
    owner_index = values // slot_count
    line_index = jnp.arange(thin_rows, dtype=jnp.int32)[None, :, None]
    placed = returned[slot_index, line_index, owner_index]
    return placed.reshape(rows_group, 1, col_total)


def solution(mesh):
    return jax.shard_map(
        body,
        mesh=mesh,
        in_specs=(P("rep", None, "fsdp", None), P("rep", "fsdp", None, None, None, None), P(), P()),
        out_specs=P("rep", "fsdp", None),
        check_vma=False,
    )
```

profile of v0, /device:TPU:1, one launch (start us, length us, event | category | flops | bytes accessed | tf_op | source)
XLA Modules:
  0.0 155.8 jit_solution(14333909433578254350)
XLA Ops:
  6.5 0.0 reduce-scatter.2.cloned.1.call-start
  6.5 0.7 reduce-scatter.2.cloned.1.call-update
  7.3 0.8 eq.31
  8.0 0.1 copy.22
  8.1 0.1 select_reduce_fusion
  8.3 0.1 reshape.278
  8.4 0.1 fusion.27
  8.5 46.5 %reduce-scatter.2.cloned.1.call-done = bf16[8,14336]{1,0:T(8,128)(2,1)} async-done(((bf16[64,14336]{1,0:T(8,128)(2,1)}), bf16[8,14336]{1,0:T(8,128)(2,1)}) %reduce-scatter.2.cloned.1.call-update) | async-done | bytes 229392 | tf_op jit(solution)/shard_map/reduce_scatter | solution.py:80
  55.0 4.6 %gather_fusion = bf16[512,512]{1,0:T(8,128)(2,1)S(1)} fusion(bf16[1,8,28,512]{3,1,2,0:T(8,128)(2,1)} %bitcast.100, s32[512]{0:T(512)S(1)} %reshape.278), kind=kCustom, calls=%fused_computation | custom fusion | bytes 1054720 | tf_op jit(solution)/shard_map/gather | solution.py:49
  59.7 0.0 copy-start.3
  59.7 1.1 fusion.21
  60.8 15.4 %all-to-all-start = ((bf16[1,8,64,512]{3,1,0,2:T(8,128)(2,1)}), bf16[1,8,64,512]{3,1,0,2:T(8,128)(2,1)S(1)}, u32[]{:S(2)}, u32[]{:S(2)}) async-start(bf16[1,8,64,512]{3,1,0,2:T(8,128)(2,1)} %fusion.21), calls=%async_computation.1 | async-start | bytes 1048576 | tf_op jit(solution)/shard_map/all_to_all | solution.py:96
  76.3 0.7 dynamic-slice.9
  76.9 0.6 dynamic-slice.10
  77.5 0.0 copy-done.3
  77.5 0.1 reshape.191
  79.3 0.6 dynamic-slice.11
  81.1 12.8 %all-to-all-done = bf16[1,8,64,512]{3,1,0,2:T(8,128)(2,1)S(1)} async-done(((bf16[1,8,64,512]{3,1,0,2:T(8,128)(2,1)}), bf16[1,8,64,512]{3,1,0,2:T(8,128)(2,1)S(1)}, u32[]{:S(2)}, u32[]{:S(2)}) %all-to-all-start) | async-done | bytes 524320 | tf_op jit(solution)/shard_map/all_to_all | solution.py:96
  94.0 2.8 %multiply_reduce_fusion.2 = (f32[]{:T(128)}, f32[512,512]{1,0:T(8,128)S(1)}) fusion(bf16[1,8,64,512]{3,1,0,2:T(8,128)(2,1)S(1)} %all-to-all-done, f32[1,2,512,512]{3,2,1,0:T(8,128)} %bitcast.106), kind=kOutput, calls=%fused_computation.42 | convolution fusion | flops 269484032 | bytes 2621444 | tf_op jit(solution)/shard_map/dot_general | solution.py:110
  97.4 0.2 fusion.18
  97.6 0.2 copy.27
  97.8 2.1 %while.48 = (s32[]{:T(128)}, bf16[512,512]{1,0:T(8,128)(2,1)S(1)}, bf16[512,512]{1,0:T(8,128)(2,1)S(1)}, bf16[512,512]{0,1:T(8,128)(2,1)S(1)}, s32[]{:T(128)}, /*index=5*/s32[]{:T(128)}) while((s32[]{:T(128)}, bf16[512,512]{1,0:T(8,128)(2,1)S(1)}, bf16[512,512]{1,0:T(8,128)(2,1)S(1)}, bf16[512,512]{0,1:T(8,128)(2,1)S(1)}, ...), condition=%wide.region_8.9_spmd.clone, body=%wide.region_7.8_spmd.clone.sunk | while | flops 1075838976 | bytes 6815813 | solution.py:29
  97.9 1.0 convolution_convert_fusion.7
  99.0 0.4 fusion.87
  99.4 0.5 convolution_bitcast_fusion.6
  99.9 0.2 copy.24
  100.1 2.4 %multiply_reduce_fusion.3 = (f32[]{:T(128)}, f32[512,512]{1,0:T(8,128)S(1)}) fusion(bf16[512,512]{1,0:T(8,128)(2,1)S(1)} %bitcast.101, f32[1,2,512,512]{3,2,1,0:T(8,128)} %bitcast.107), kind=kOutput, calls=%fused_computation.44 | convolution fusion | flops 269484032 | bytes 3145732 | tf_op jit(solution)/shard_map/dot_general | solution.py:107
  103.1 1.0 fusion.16
  104.1 1.3 copy.25
  105.4 4.2 %while.47 = (s32[]{:T(128)}, bf16[512,512]{1,0:T(8,128)(2,1)S(1)}, bf16[512,512]{1,0:T(8,128)(2,1)}, bf16[512,512]{0,1:T(8,128)(2,1)S(1)}, s32[]{:T(128)}, /*index=5*/s32[]{:T(128)}) while((s32[]{:T(128)}, bf16[512,512]{1,0:T(8,128)(2,1)S(1)}, bf16[512,512]{1,0:T(8,128)(2,1)}, bf16[512,512]{0,1:T(8,128)(2,1)S(1)}, s32[]{:T(128)}, ...), condition=%wide.region_5.6_spmd.clone, body=%wide.region_4.5_spmd.clone.sunk | while | flops 1075838976 | bytes 8912993 | solution.py:29
  105.5 2.9 %convolution_convert_fusion.6 = bf16[512,512]{1,0:T(8,128)(2,1)S(1)} fusion(bf16[512,512]{1,0:T(8,128)(2,1)} %get-tuple-element.330), kind=kOutput, calls=%fused_computation.5.clone.1 | convolution fusion | flops 537395200 | bytes 1048576 | tf_op jit(solution)/shard_map/while/body/eval_jaxpr/while/body/dot_general | solution.py:19
  108.4 0.4 fusion.80
  108.8 0.0 copy-start.2
  108.8 0.5 convolution_bitcast_fusion.5
  109.3 0.3 copy-done.2
  109.6 0.5 fusion.41
  110.1 1.8 %multiply_reduce_fusion = (f32[]{:T(128)}, f32[512,512]{1,0:T(8,128)S(1)}) fusion(f32[512,512]{1,0:T(8,128)S(1)} %fusion.41, bf16[512,512]{0,1:T(8,128)(2,1)S(1)} %get-tuple-element.96), kind=kOutput, calls=%fused_computation.40 | convolution fusion | flops 1611137024 | bytes 2621444 | tf_op jit(solution)/shard_map/dot_general | solution.py:54
  112.5 0.0 copy-done.1
  112.5 0.9 multiply_reduce_fusion.1
  114.1 0.1 multiply_convert_fusion
  114.2 1.1 copy.28
  115.3 12.0 %all-to-all-start.1 = ((bf16[1,8,64,512]{3,1,0,2:T(8,128)(2,1)}), bf16[1,8,64,512]{3,1,0,2:T(8,128)(2,1)S(1)}, u32[]{:S(2)}, u32[]{:S(2)}) async-start(bf16[1,8,64,512]{3,1,0,2:T(8,128)(2,1)} %copy.28), calls=%async_computation.2 | async-start | bytes 1048576 | tf_op jit(solution)/shard_map/all_to_all | solution.py:122
  127.4 0.1 add_bitcast_fusion.1
  127.4 0.1 reshape.286
  127.5 17.5 %all-to-all-done.1 = bf16[1,8,64,512]{3,1,0,2:T(8,128)(2,1)S(1)} async-done(((bf16[1,8,64,512]{3,1,0,2:T(8,128)(2,1)}), bf16[1,8,64,512]{3,1,0,2:T(8,128)(2,1)S(1)}, u32[]{:S(2)}, u32[]{:S(2)}) %all-to-all-start.1) | async-done | bytes 524320 | tf_op jit(solution)/shard_map/all_to_all | solution.py:122
  145.0 0.2 copy.29
  145.2 2.8 %gather_fusion.1 = bf16[224,512]{1,0:T(8,128)(2,1)S(1)} fusion(bf16[1,8,64,512]{3,2,1,0:T(8,128)(2,1)S(1)} %copy.29, s32[224]{0:T(256)S(1)} %reshape.286), kind=kCustom, calls=%fused_computation.1 | custom fusion | bytes 461440 | tf_op jit(solution)/shard_map/gather | solution.py:133
  147.9 1.0 reshape.194
  (19 shorter events, 0.2 us)
Async XLA Ops:
  6.5 48.5 %reduce-scatter.2.cloned.1.call-start = ((), (), s32[]{:S(2)}) async-start(), calls=%async_computation.3 | async-start | bytes 2064384 | tf_op jit(solution)/shard_map/reduce_scatter | solution.py:80
  59.7 17.8 %copy-start.3 = (s32[224]{0:T(256)S(1)}, s32[224]{0:T(256)}, u32[]{:S(2)}) copy-start(s32[224]{0:T(256)} %param.11) | copy-start | bytes 2692
  60.8 33.1 %all-to-all-start = ((bf16[1,8,64,512]{3,1,0,2:T(8,128)(2,1)}), bf16[1,8,64,512]{3,1,0,2:T(8,128)(2,1)S(1)}, u32[]{:S(2)}, u32[]{:S(2)}) async-start(bf16[1,8,64,512]{3,1,0,2:T(8,128)(2,1)} %fusion.21), calls=%async_computation.1 | async-start | bytes 1048576 | tf_op jit(solution)/shard_map/all_to_all | solution.py:96
  94.0 5.9 %copy-start = (bf16[1,8,64,512]{3,1,0,2:T(8,128)(2,1)}, bf16[1,8,64,512]{3,1,0,2:T(8,128)(2,1)S(1)}, u32[]{:S(2)}) copy-start(bf16[1,8,64,512]{3,1,0,2:T(8,128)(2,1)S(1)} %all-to-all-done) | copy-start | bytes 1572868
  108.8 0.8 copy-start.2
  109.6 2.9 %copy-start.1 = (bf16[1,8,64,512]{3,1,0,2:T(8,128)(2,1)S(1)}, bf16[1,8,64,512]{3,1,0,2:T(8,128)(2,1)}, u32[]{:S(2)}) copy-start(bf16[1,8,64,512]{3,1,0,2:T(8,128)(2,1)} %copy-done) | copy-start | bytes 1572868
  115.3 29.7 %all-to-all-start.1 = ((bf16[1,8,64,512]{3,1,0,2:T(8,128)(2,1)}), bf16[1,8,64,512]{3,1,0,2:T(8,128)(2,1)S(1)}, u32[]{:S(2)}, u32[]{:S(2)}) async-start(bf16[1,8,64,512]{3,1,0,2:T(8,128)(2,1)} %copy.28), calls=%async_computation.2 | async-start | bytes 1048576 | tf_op jit(solution)/shard_map/all_to_all | solution.py:122
Sparse Core Ops, SparseCore 0:
  10.2 44.7 reduce-scatter.1
where the time goes:
time: 156 us
  waiting for transfers between devices  77.6 us (50%)
  starting transfers between devices  27.4 us (18%)
  between operations  19.2 us (12%)
  local copies, waits for them, and re-layouts  14.7 us (9%)
  matrix products  13.1 us (8%)
  other arithmetic  3.63 us (2%)
    reduce_scatter x1, waiting for transfers between devices, body(): lax.psum_scatter(partial_value.astype(jnp.float32).astype(jnp.bfloat16),...  46.5 us
    all_to_all x1, waiting for transfers between devices, body(): lax.all_to_all(scaled.reshape(slot_count, thin_rows, fsdp_count, block_si...  17.5 us
    all_to_all x1, starting transfers between devices, body(): lax.all_to_all(outgoing.astype(jnp.bfloat16), 'fsdp', split_axis=2, conca...  15.4 us
    all_to_all x1, waiting for transfers between devices, body(): lax.all_to_all(outgoing.astype(jnp.bfloat16), 'fsdp', split_axis=2, conca...  12.8 us
    all_to_all x1, starting transfers between devices, body(): lax.all_to_all(scaled.reshape(slot_count, thin_rows, fsdp_count, block_si...  12 us
    gather x1, local copies, waits for them, and re-layouts, pack_pieces(): picked = grid_view[band_index, line_index, col_index]  4.62 us
    dot_general x2, matrix products, advance(): jnp.dot(square_t, square_t, preferred_element_type=jnp.float32)  3.91 us
  transfers between devices with their start and end apart: 3, of which 3 were waited for; matrix products, arithmetic and copies ran while one was open for 2% of the time, Pallas kernels for 0%

commit v1 on v0

v1 whole, which is shorter than its diff:
```python
import functools

import jax
import jax.numpy as jnp
from jax import lax
from jax.experimental import pallas as pl
from jax.experimental.pallas import tpu as pltpu
from jax.sharding import PartitionSpec as P

F32 = jnp.float32
BF16 = jnp.bfloat16
PARTS = 2


def mm(a, b, dims=((1,), (0,))):
    return lax.dot_general(a, b, (dims, ((), ())), preferred_element_type=F32)


def kernel(
    n_rep, n_fsdp, n_col,
    x_hbm, s_hbm, owner_ref, count_ref, out_ref,
    x_v, s_v, ring_out, ring_in, summed, packed, g_in, g_f, g_n, d_f, d_out, d_in,
    blk_v, blk_s,
    x_sem, s_sem, blk_sem, ring_send, ring_recv, fwd_send, fwd_recv, back_send, back_recv,
):
    rep = lax.axis_index("rep")
    me = lax.axis_index("fsdp")
    block = s_v.shape[-1]
    width = block // PARTS
    half = n_col // 2
    far = n_rep // 2
    up = lax.rem(rep + 1, n_rep)
    down = lax.rem(rep + n_rep - 1, n_rep)

    barrier = pltpu.get_barrier_semaphore()
    for peer in (up, down):
        pl.semaphore_signal(barrier, inc=1, device_id={"rep": peer}, device_id_type=pl.DeviceIdType.MESH)

    def greet(t, carry):
        w = lax.rem(me + t, n_fsdp)
        pl.semaphore_signal(barrier, inc=1, device_id={"fsdp": w}, device_id_type=pl.DeviceIdType.MESH)
        return carry

    lax.fori_loop(1, n_fsdp, greet, 0)

    def x_copy(k):
        d = lax.rem(rep + k, n_rep)
        return pltpu.make_async_copy(x_hbm.at[d], x_v.at[d], x_sem.at[k])

    order = [far]
    for k in range(far - 1, 0, -1):
        order += [k, n_rep - k]
    order.append(0)
    for k in order:
        x_copy(k).start()
    s_copy = pltpu.make_async_copy(s_hbm, s_v, s_sem)
    s_copy.start()

    lanes = lax.broadcasted_iota(jnp.int32, blk_v.shape, 1)
    slots = jnp.zeros(blk_v.shape, jnp.int32)
    for j in range(n_col):
        slots = jnp.where(lanes == owner_ref[rep * n_col + j], j, slots)
    blk_v[...] = slots
    blk_copy = pltpu.make_async_copy(blk_v, blk_s, blk_sem)
    blk_copy.start()
    x_copy(far).wait()
    pl.semaphore_wait(barrier, n_fsdp + 1)

    def own(k, j, c):
        d = lax.rem(rep + k, n_rep)
        start = pl.multiple_of(j * block + c * width, 128)
        return x_v[d, :, pl.ds(start, width)]

    def ring_copy(way, s, c):
        lo = half * way if s == 0 else 0
        size = half if s == 0 else n_col
        return pltpu.make_async_remote_copy(
            src_ref=ring_out.at[way, s, c, pl.ds(lo, size)],
            dst_ref=ring_in.at[way, s, c, pl.ds(lo, size)],
            send_sem=ring_send.at[way, s, c],
            recv_sem=ring_recv.at[way, s, c],
            device_id={"rep": up if way == 0 else down},
            device_id_type=pl.DeviceIdType.MESH,
        )

    waited = {far}

    def ring_step(s, c):
        for way in range(2):
            k = far - s if way == 0 else n_rep - far + s
            if k not in waited:
                waited.add(k)
                x_copy(k).wait()
            if s > 0:
                ring_copy(way, s - 1, c).wait_recv()

            def add(j, carry):
                total = ring_in[way, s - 1, c, j].astype(F32) + own(k, j, c).astype(F32)
                ring_out[way, s, c, j] = total.astype(BF16)
                return carry

            def keep(j, carry):
                ring_out[way, s, c, j] = own(k, j, c)
                return carry

            lo = half * way
            other = half - lo
            if s == 0:
                lax.fori_loop(lo, lo + half, keep, 0)
            elif s == 1:
                lax.fori_loop(lo, lo + half, add, 0)
                lax.fori_loop(other, other + half, keep, 0)
            else:
                lax.fori_loop(0, n_col, add, 0)
            ring_copy(way, s, c).start()

    def fwd_copy(w, c):
        return pltpu.make_async_remote_copy(
            src_ref=packed.at[c, w],
            dst_ref=g_in.at[c, me],
            send_sem=fwd_send.at[c],
            recv_sem=fwd_recv.at[c],
            device_id={"fsdp": w},
            device_id_type=pl.DeviceIdType.MESH,
        )

    def finish(c):
        if 0 not in waited:
            waited.add(0)
            x_copy(0).wait()
        for way in range(2):
            ring_copy(way, far - 1, c).wait_recv()

        def add(j, carry):
            total = own(0, j, c).astype(F32)
            for way in range(2):
                total = total + ring_in[way, far - 1, c, j].astype(F32)
            summed[c, j] = total.astype(BF16)
            return carry

        lax.fori_loop(0, n_col, add, 0)

        def send(t, carry):
            w = lax.rem(me + t, n_fsdp)
            packed[c, w] = summed[c, blk_s[0, w]]
            fwd_copy(w, c).start()
            return carry

        lax.fori_loop(1, n_fsdp, send, 0)
        g_in[c, me] = summed[c, blk_s[0, me]]

    blk_copy.wait()
    for s in range(far):
        for c in range(PARTS):
            ring_step(s, c)
    for c in range(PARTS):
        finish(c)

    s_copy.wait()
    for c in range(PARTS):
        filled = g_in.at[c, pl.ds(0, n_fsdp - 1)]
        pltpu.make_async_copy(filled, filled, fwd_recv.at[c]).wait()
        lines = g_in[c].astype(F32).reshape(block, width)
        for q in range(width // 128):
            g_f[c * (width // 128) + q] = lines[:, q * 128:(q + 1) * 128]
    thin = block // n_fsdp
    for q in range(block // 128):
        for a in range(thin):
            g_n[a * n_fsdp:(a + 1) * n_fsdp, q * 128:(q + 1) * 128] = g_f[
                q, pl.ds(a, n_fsdp, stride=thin), :
            ].astype(BF16)

    grad = g_n[...]
    grad32 = grad.astype(F32)
    grad_mass = jnp.sum(grad32 * grad32)
    stats = [
        0.9 * s_v[0] + mm(grad, grad, ((1,), (1,))),
        0.9 * s_v[1] + mm(grad, grad, ((0,), (0,))),
    ]
    row = lax.broadcasted_iota(jnp.int32, (block, block), 0)
    col = lax.broadcasted_iota(jnp.int32, (block, block), 1)
    five = jnp.where(row == col, 1.25, 0.0)
    more = count_ref[rep * n_col + blk_s[0, me]] > 2

    newton = [a * (1.0 / jnp.sqrt(jnp.sum(a * a) + 1e-6)) for a in stats]
    step = [(five - 0.25 * m).astype(BF16) for m in newton]
    newton = [m.astype(BF16) for m in newton]
    power = list(step)
    first = None
    for it in range(2):
        square = [mm(t, t).astype(BF16) for t in step]
        fourth = [mm(t, t).astype(BF16) for t in square]
        newton32 = [mm(fourth[i], newton[i]) for i in range(2)]
        step = [(five - 0.25 * m).astype(BF16) for m in newton32]
        newton = [m.astype(BF16) for m in newton32]
        power = [mm(power[i], step[i]).astype(BF16) for i in range(2)]
        if it == 0:
            first = power
    roots = [jnp.where(more, power[i], first[i]) for i in range(2)]
    halfway = mm(roots[0], grad).astype(BF16)
    precond = mm(halfway, roots[1])
    pre_mass = jnp.sum(precond * precond)
    scaled = precond * jnp.sqrt(grad_mass / (pre_mass + 1e-6))
    for q in range(block // 128):
        d_f[q] = scaled[:, q * 128:(q + 1) * 128]

    def back_copy(w):
        return pltpu.make_async_remote_copy(
            src_ref=d_out.at[w],
            dst_ref=d_in.at[me],
            send_sem=back_send,
            recv_sem=back_recv,
            device_id={"fsdp": w},
            device_id_type=pl.DeviceIdType.MESH,
        )

    def lines_of(w):
        return jnp.concatenate(
            [d_f[q, pl.ds(w, thin, stride=n_fsdp), :] for q in range(block // 128)], axis=1
        ).astype(BF16)

    def send_back(t, carry):
        w = lax.rem(me + t, n_fsdp)
        d_out[w] = lines_of(w)
        back_copy(w).start()
        return carry

    lax.fori_loop(1, n_fsdp, send_back, 0)
    d_in[me] = lines_of(me)

    filled = d_in.at[pl.ds(0, n_fsdp - 1)]
    pltpu.make_async_copy(filled, filled, back_recv).wait()
    for j in range(n_col):
        out_ref[:, j * block:(j + 1) * block] = d_in[owner_ref[rep * n_col + j]]

    for way in range(2):
        for s in range(far):
            for c in range(PARTS):
                ring_copy(way, s, c).wait_send()
    for c in range(PARTS):
        sent = packed.at[c, pl.ds(0, n_fsdp - 1)]
        pltpu.make_async_copy(sent, sent, fwd_send.at[c]).wait()
    sent = d_out.at[pl.ds(0, n_fsdp - 1)]
    pltpu.make_async_copy(sent, sent, back_send).wait()


def body(grad_partials, stats_prev, owner_table, newton_counts):
    n_rep = lax.axis_size("rep")
    n_fsdp = lax.axis_size("fsdp")
    cols = grad_partials.shape[3]
    block = stats_prev.shape[-1]
    n_col = cols // block
    lines = grad_partials.shape[1] // n_rep
    far = n_rep // 2
    width = block // PARTS
    x = grad_partials.reshape(n_rep, lines, cols)
    s = stats_prev.reshape(2, block, block)
    out = pl.pallas_call(
        functools.partial(kernel, n_rep, n_fsdp, n_col),
        out_shape=jax.ShapeDtypeStruct((lines, cols), BF16),
        in_specs=[
            pl.BlockSpec(memory_space=pl.ANY),
            pl.BlockSpec(memory_space=pl.ANY),
            pl.BlockSpec(memory_space=pltpu.SMEM),
            pl.BlockSpec(memory_space=pltpu.SMEM),
        ],
        out_specs=pl.BlockSpec(memory_space=pltpu.VMEM),
        scratch_shapes=[
            pltpu.VMEM((n_rep, lines, cols), BF16),
            pltpu.VMEM((2, block, block), F32),
            pltpu.VMEM((2, far, PARTS, n_col, lines, width), BF16),
            pltpu.VMEM((2, far, PARTS, n_col, lines, width), BF16),
            pltpu.VMEM((PARTS, n_col, lines, width), BF16),
            pltpu.VMEM((PARTS, n_fsdp, lines, width), BF16),
            pltpu.VMEM((PARTS, n_fsdp, lines, width), BF16),
            pltpu.VMEM((block // 128, block, 128), F32),
            pltpu.VMEM((block, block), BF16),
            pltpu.VMEM((block // 128, block, 128), F32),
            pltpu.VMEM((n_fsdp, lines, block), BF16),
            pltpu.VMEM((n_fsdp, lines, block), BF16),
            pltpu.VMEM((8, 128), jnp.int32),
            pltpu.SMEM((8, 128), jnp.int32),
            pltpu.SemaphoreType.DMA((n_rep,)),
            pltpu.SemaphoreType.DMA,
            pltpu.SemaphoreType.DMA,
            pltpu.SemaphoreType.DMA((2, far, PARTS)),
            pltpu.SemaphoreType.DMA((2, far, PARTS)),
            pltpu.SemaphoreType.DMA((PARTS,)),
            pltpu.SemaphoreType.DMA((PARTS,)),
            pltpu.SemaphoreType.DMA,
            pltpu.SemaphoreType.DMA,
        ],
        compiler_params=pltpu.CompilerParams(
            collective_id=0, has_side_effects=True, vmem_limit_bytes=48 * 1024 * 1024
        ),
        cost_estimate=pl.CostEstimate(
            flops=40 * block**3, bytes_accessed=6 * 1024 * 1024, transcendentals=0
        ),
    )(x, s, owner_table, newton_counts)
    return out.reshape(lines, 1, cols)


def solution(mesh):
    return jax.shard_map(
        body,
        mesh=mesh,
        in_specs=(P("rep", None, "fsdp", None), P("rep", "fsdp", None, None, None, None), P(), P()),
        out_specs=P("rep", "fsdp", None),
        check_vma=False,
    )
```

time: 156 us -> 76.8 us (0.49)
  waiting for transfers between devices: 77.6 us -> 0 us
  Pallas kernels: 0 us -> 71.4 us
  starting transfers between devices: 27.4 us -> 0 us
  between operations: 19.2 us -> 0.01 us
  matrix products: 13.1 us -> 0 us
  local copies, waits for them, and re-layouts: 14.7 us -> 5.14 us
  other arithmetic: 3.63 us -> 0 us
    pallas_call x0 -> x1, Pallas kernels: none -> 71.4 us  [body(): pl.pallas_call(functools.partial(kernel, n_rep, n_fsdp, n_col), out_shape...]
    reduce_scatter x1 -> x0, waiting for transfers between devices: 46.5 us -> none  [body(): lax.psum_scatter(partial_value.astype(jnp.float32).astype(jnp.bfloat16),...]
    all_to_all x2 -> x0, waiting for transfers between devices: 30.3 us -> none  [the longest x1 17.5 us: body(): lax.all_to_all(scaled.reshape(slot_count, thin_rows, fsdp_count, block_si...]
    all_to_all x2 -> x0, starting transfers between devices: 27.4 us -> none  [the longest x1 15.4 us: body(): lax.all_to_all(outgoing.astype(jnp.bfloat16), 'fsdp', split_axis=2, conca...]
    dot_general x10 -> x0, matrix products: 13.1 us -> none  [the longest x2 3.91 us: advance(): jnp.dot(square_t, square_t, preferred_element_type=jnp.float32)]
    gather x5 -> x0, local copies, waits for them, and re-layouts: 9.23 us -> none  [the longest x1 4.62 us: pack_pieces(): picked = grid_view[band_index, line_index, col_index]]
    unnamed x8 -> x9, local copies, waits for them, and re-layouts: 1.48 us -> 5.14 us
    convert_element_type x4 -> x0, other arithmetic: 2.43 us -> none  [the longest x2 1.17 us: inverse_root(): step_t = ((5.0 * identity - newton_m) * 0.25).astype(jnp.bfloat16)]
  transfers between devices with their start and end apart: 3 -> 0, of which waited for: 3 -> 0; matrix products, arithmetic and copies ran while one was open for 2% -> 0% of each run, Pallas kernels for 0% -> 0%
where the time goes in v1:
time: 76.8 us; the launch traced here: 76.6 us
  Pallas kernels  71.4 us (93%)
  local copies, waits for them, and re-layouts  5.14 us (7%)
    pallas_call x1, Pallas kernels, body(): pl.pallas_call(functools.partial(kernel, n_rep, n_fsdp, n_col), out_shape...  71.4 us
    unnamed x9, local copies, waits for them, and re-layouts  5.14 us

profile of v1, /device:TPU:1, one launch (start us, length us, event | category | flops | bytes accessed | tf_op | source)
XLA Modules:
  0.0 76.6 jit_solution(16862624191404626511)
XLA Ops:
  0.0 0.0 copy-start
  0.0 1.6 %copy-done = f32[1,1,1,2,512,512]{5,4,3,2,1,0:T(8,128)S(1)} copy-done((f32[1,1,1,2,512,512]{5,4,3,2,1,0:T(8,128)S(1)}, f32[1,1,1,2,512,512]{5,4,3,2,1,0:T(8,128)}, u32[]{:S(2)}) %copy-start) | copy-done | bytes 2097176
  1.6 0.0 copy-start.1
  1.6 1.5 %copy-done.1 = bf16[1,64,1,14336]{3,1,2,0:T(8,128)(2,1)S(1)} copy-done((bf16[1,64,1,14336]{3,1,2,0:T(8,128)(2,1)S(1)}, bf16[1,64,1,14336]{3,1,2,0:T(8,128)(2,1)}, u32[]{:S(2)}) %copy-start.1) | copy-done | bytes 1835032
  3.1 0.0 copy-start.2
  3.1 0.7 copy-done.2
  3.8 0.0 copy-start.3
  3.8 0.7 copy-done.3
  4.5 71.4 %shard_map.46 = bf16[8,14336]{1,0:T(8,128)(2,1)S(1)} custom-call(bf16[8,8,14336]{2,1,0:T(8,128)(2,1)S(1)} %bitcast.5, f32[2,512,512]{2,1,0:T(8,128)S(1)} %bitcast.4, s32[224]{0:T(256)S(1)} %copy-done.2, s32[224]{0:T(256)S(1)} %copy-done.3), custom_call_target="tpu_custom_call" | custom-call | flops 5368709120 | bytes 6291456 | tf_op jit(solution)/shard_map/pallas_call | solution.py:258
  75.9 0.7 copy.6
Async XLA Ops:
  0.0 1.6 %copy-start = (f32[1,1,1,2,512,512]{5,4,3,2,1,0:T(8,128)S(1)}, f32[1,1,1,2,512,512]{5,4,3,2,1,0:T(8,128)}, u32[]{:S(2)}) copy-start(f32[1,1,1,2,512,512]{5,4,3,2,1,0:T(8,128)} %param.5) | copy-start | bytes 6291460
  1.6 1.5 %copy-start.1 = (bf16[1,64,1,14336]{3,1,2,0:T(8,128)(2,1)S(1)}, bf16[1,64,1,14336]{3,1,2,0:T(8,128)(2,1)}, u32[]{:S(2)}) copy-start(bf16[1,64,1,14336]{3,1,2,0:T(8,128)(2,1)} %param.4) | copy-start | bytes 5505028
  3.1 0.7 copy-start.2
  3.8 0.7 copy-start.3

commit v2 on v1

v2 whole, which is shorter than its diff:
```python
import functools

import jax
import jax.numpy as jnp
from jax import lax
from jax.experimental import pallas as pl
from jax.experimental.pallas import tpu as pltpu
from jax.sharding import PartitionSpec as P

F32 = jnp.float32
BF16 = jnp.bfloat16
PARTS = 2
INNER = 8
DEPTH = 2
GROUP = 14


def mm(a, b, dims=((1,), (0,))):
    return lax.dot_general(a, b, (dims, ((), ())), preferred_element_type=F32)


def kernel(
    n_rep, n_fsdp, n_col,
    x_hbm, s_hbm, owner_ref, count_ref, out_ref,
    x_v, s_v, ring_out, ring_in, summed, packed, g_in, g_f, g_n, d_f, d_out, d_in,
    blk_v, blk_s,
    x_sem, s_sem, blk_sem, ring_send, ring_recv, fwd_send, fwd_recv, back_send, back_recv, near_sem,
):
    rep = lax.axis_index("rep")
    me = lax.axis_index("fsdp")
    outer = n_fsdp // INNER
    plane = me // INNER
    place = lax.rem(me, INNER)
    block = s_v.shape[-1]
    width = block // PARTS
    groups = n_col // GROUP
    far = n_rep // 2
    thin = block // n_fsdp
    up = lax.rem(rep + 1, n_rep)
    down = lax.rem(rep + n_rep - 1, n_rep)

    barrier = pltpu.get_barrier_semaphore()

    def greet(sem, **peer):
        pl.semaphore_signal(sem, inc=1, device_id=peer, device_id_type=pl.DeviceIdType.MESH)

    def greet_planes(t, carry):
        greet(barrier, fsdp=lax.rem(plane + t, outer) * INNER + place)
        return carry

    def greet_places(t, carry):
        greet(barrier, fsdp=plane * INNER + lax.rem(place + t, INNER))
        return carry

    def greet_near(t, carry):
        greet(near_sem, fsdp=plane * INNER + lax.rem(place + t, INNER))
        return carry

    def x_copy(k):
        d = lax.rem(rep + k, n_rep)
        return pltpu.make_async_copy(x_hbm.at[d], x_v.at[d], x_sem.at[k])

    order = [far]
    for k in range(far - 1, 0, -1):
        order += [k, n_rep - k]
    order.append(0)

    x_copy(far).start()
    greet(barrier, rep=up)
    greet(barrier, rep=down)
    lax.fori_loop(1, outer, greet_planes, 0)
    lax.fori_loop(1, INNER, greet_places, 0)
    for k in order[1:]:
        x_copy(k).start()
    s_copy = pltpu.make_async_copy(s_hbm, s_v, s_sem)
    s_copy.start()

    lanes = lax.broadcasted_iota(jnp.int32, blk_v.shape, 1)
    slots = jnp.zeros(blk_v.shape, jnp.int32)
    for j in range(n_col):
        slots = jnp.where(lanes == owner_ref[rep * n_col + j], j, slots)
    blk_v[...] = slots
    blk_copy = pltpu.make_async_copy(blk_v, blk_s, blk_sem)
    blk_copy.start()

    def own(k, j, p):
        d = lax.rem(rep + k, n_rep)
        return x_v[d, :, j * block + p * width:j * block + (p + 1) * width]

    def ring_copy(way, s, p, g):
        return pltpu.make_async_remote_copy(
            src_ref=ring_out.at[way, s, p, pl.ds(g * GROUP, GROUP)],
            dst_ref=ring_in.at[way, s, p, pl.ds(g * GROUP, GROUP)],
            send_sem=ring_send.at[way, s, p, g],
            recv_sem=ring_recv.at[way, s, p, g],
            device_id={"rep": up if way == 0 else down},
            device_id_type=pl.DeviceIdType.MESH,
        )

    waited = set()

    def x_wait(k):
        if k not in waited:
            waited.add(k)
            x_copy(k).wait()

    def starts(way, g):
        return (g < groups // 2) == (way == 0)

    flight = ([], [])

    def ring_step(way, s, p, g):
        k = far - s if way == 0 else n_rep - far + s
        x_wait(k)
        joined = s > 1 or (s == 1 and starts(way, g))
        if joined:
            ring_copy(way, s - 1, p, g).wait_recv()
        for j in range(g * GROUP, (g + 1) * GROUP):
            mine = own(k, j, p)
            ring_out[way, s, p, j] = ring_in[way, s - 1, p, j] + mine if joined else mine
        if len(flight[way]) == DEPTH:
            flight[way].pop(0).wait_send()
        flight[way].append(ring_copy(way, s, p, g))
        flight[way][-1].start()

    def finish(p, g):
        x_wait(0)
        for way in range(2):
            ring_copy(way, far - 1, p, g).wait_recv()
        for j in range(g * GROUP, (g + 1) * GROUP):
            total = own(0, j, p).astype(F32)
            for way in range(2):
                total = total + ring_in[way, far - 1, p, j].astype(F32)
            summed[p, j] = total.astype(BF16)

    def fwd_copy(w, p):
        return pltpu.make_async_remote_copy(
            src_ref=packed.at[p, w],
            dst_ref=g_in.at[p, me],
            send_sem=fwd_send.at[p],
            recv_sem=fwd_recv.at[p],
            device_id={"fsdp": w},
            device_id_type=pl.DeviceIdType.MESH,
        )

    def forward(p, lo, hi):
        def send(t, carry):
            w = lax.rem(me + t, n_fsdp)
            packed[p, w] = summed[p, blk_s[0, w]]
            fwd_copy(w, p).start()
            return carry

        lax.fori_loop(lo, hi, send, 0)

    def await_bytes(sem, buffer):
        part = buffer.at[pl.ds(0, n_fsdp - 1)]
        pltpu.make_async_copy(part, part, sem).wait()

    def gather(p):
        g_in[p, me] = summed[p, blk_s[0, me]]
        await_bytes(fwd_recv.at[p], g_in.at[p])
        lines = g_in[p].astype(F32).reshape(block, width)
        for q in range(width // 128):
            at = p * (width // 128) + q
            g_f[at] = lines[:, q * 128:(q + 1) * 128]
            for a in range(thin):
                g_n[p, a * n_fsdp:(a + 1) * n_fsdp, q * 128:(q + 1) * 128] = g_f[
                    at, pl.ds(a, n_fsdp, stride=thin), :
                ].astype(BF16)

    def drain():
        for way in range(2):
            for copy in flight[way]:
                copy.wait_send()
        for p in range(PARTS):
            await_bytes(fwd_send.at[p], packed.at[p])
        await_bytes(back_send, d_out)

    x_wait(far)
    blk_copy.wait()
    pl.semaphore_wait(barrier, outer + INNER)

    def pairs(p, s, kind):
        first = [[g for g in range(groups) if starts(way, g)] for way in range(2)]
        rest = [[g for g in range(groups) if not starts(way, g)] for way in range(2)]
        picked = [{"first": first, "rest": rest, "all": [rest[i] + first[i] for i in range(2)]}[kind][i] for i in range(2)]
        return [[(0, s, p, g), (1, s, p, h)] for g, h in zip(*picked)]

    def steps(p):
        return [pairs(p, 0, "first"), pairs(p, 1, "rest"), pairs(p, 1, "first")] + [
            pairs(p, s, "all") for s in range(2, far)
        ]

    def run(list_of_pairs):
        for pair in list_of_pairs:
            for step in pair:
                ring_step(*step)

    part0, part1 = steps(0), steps(1)
    run(part0[0])
    lax.fori_loop(1, INNER, greet_near, 0)
    run(part1[0])
    for a, b in zip(part0[1:], part1[1:]):
        run(a)
        run(b)
    pl.semaphore_wait(near_sem, INNER - 1)
    for p in range(PARTS):
        for g in range(groups):
            finish(p, g)
        forward(p, 1, n_fsdp)
    s_copy.wait()
    gather(0)
    left = g_n[0]
    grad32 = left.astype(F32)
    grad_mass = jnp.sum(grad32 * grad32)
    s_v[0] = 0.9 * s_v[0] + mm(left, left, ((1,), (1,)))
    s_v[1] = 0.9 * s_v[1]
    s_v[1, :width, :width] = s_v[1, :width, :width] + mm(left, left, ((0,), (0,)))
    gather(1)
    right = g_n[1]
    grad32 = right.astype(F32)
    grad_mass = grad_mass + jnp.sum(grad32 * grad32)
    across = mm(left, right, ((0,), (0,)))
    stats = [
        s_v[0] + mm(right, right, ((1,), (1,))),
        s_v[1] + jnp.concatenate(
            [
                jnp.concatenate([jnp.zeros((width, width), F32), across], axis=1),
                jnp.concatenate([mm(right, left, ((0,), (0,))), mm(right, right, ((0,), (0,)))], axis=1),
            ],
            axis=0,
        ),
    ]
    grad = jnp.concatenate([left, right], axis=1)
    row = lax.broadcasted_iota(jnp.int32, (block, block), 0)
    col = lax.broadcasted_iota(jnp.int32, (block, block), 1)
    five = jnp.where(row == col, 1.25, 0.0)
    more = count_ref[rep * n_col + blk_s[0, me]] > 2

    newton = [a * (1.0 / jnp.sqrt(jnp.sum(a * a) + 1e-6)) for a in stats]
    step = [(five - 0.25 * m).astype(BF16) for m in newton]
    newton = [m.astype(BF16) for m in newton]
    power = list(step)
    first = None
    for it in range(2):
        square = [mm(t, t).astype(BF16) for t in step]
        fourth = [mm(t, t).astype(BF16) for t in square]
        newton32 = [mm(fourth[i], newton[i]) for i in range(2)]
        step = [(five - 0.25 * m).astype(BF16) for m in newton32]
        newton = [m.astype(BF16) for m in newton32]
        power = [mm(power[i], step[i]).astype(BF16) for i in range(2)]
        if it == 0:
            first = power
    roots = [jnp.where(more, power[i], first[i]) for i in range(2)]
    halfway = mm(roots[0], grad).astype(BF16)
    precond = mm(halfway, roots[1])
    pre_mass = jnp.sum(precond * precond)
    scaled = precond * jnp.sqrt(grad_mass / (pre_mass + 1e-6))
    for q in range(block // 128):
        d_f[q] = scaled[:, q * 128:(q + 1) * 128]

    def back_copy(w):
        return pltpu.make_async_remote_copy(
            src_ref=d_out.at[w],
            dst_ref=d_in.at[me],
            send_sem=back_send,
            recv_sem=back_recv,
            device_id={"fsdp": w},
            device_id_type=pl.DeviceIdType.MESH,
        )

    def lines_of(w):
        return jnp.concatenate(
            [d_f[q, pl.ds(w, thin, stride=n_fsdp), :] for q in range(block // 128)], axis=1
        ).astype(BF16)

    def send_back(t, carry):
        w = lax.rem(me + t, n_fsdp)
        d_out[w] = lines_of(w)
        back_copy(w).start()
        return carry

    def send_both(i, carry):
        send_back(n_fsdp // 2 - i, carry)
        return send_back(n_fsdp // 2 + i, carry)

    send_back(n_fsdp // 2, 0)
    lax.fori_loop(1, n_fsdp // 2, send_both, 0)
    d_in[me] = lines_of(me)

    await_bytes(back_recv, d_in)
    for j in range(n_col):
        out_ref[:, j * block:(j + 1) * block] = d_in[owner_ref[rep * n_col + j]]

    drain()


def body(grad_partials, stats_prev, owner_table, newton_counts):
    n_rep = lax.axis_size("rep")
    n_fsdp = lax.axis_size("fsdp")
    cols = grad_partials.shape[3]
    block = stats_prev.shape[-1]
    n_col = cols // block
    lines = grad_partials.shape[1] // n_rep
    far = n_rep // 2
    width = block // PARTS
    x = grad_partials.reshape(n_rep, lines, cols)
    s = stats_prev.reshape(2, block, block)
    out = pl.pallas_call(
        functools.partial(kernel, n_rep, n_fsdp, n_col),
        out_shape=jax.ShapeDtypeStruct((lines, cols), BF16),
        in_specs=[
            pl.BlockSpec(memory_space=pl.ANY),
            pl.BlockSpec(memory_space=pl.ANY),
            pl.BlockSpec(memory_space=pltpu.SMEM),
            pl.BlockSpec(memory_space=pltpu.SMEM),
        ],
        out_specs=pl.BlockSpec(memory_space=pltpu.VMEM),
        scratch_shapes=[
            pltpu.VMEM((n_rep, lines, cols), BF16),
            pltpu.VMEM((2, block, block), F32),
            pltpu.VMEM((2, far, PARTS, n_col, lines, width), BF16),
            pltpu.VMEM((2, far, PARTS, n_col, lines, width), BF16),
            pltpu.VMEM((PARTS, n_col, lines, width), BF16),
            pltpu.VMEM((PARTS, n_fsdp, lines, width), BF16),
            pltpu.VMEM((PARTS, n_fsdp, lines, width), BF16),
            pltpu.VMEM((block // 128, block, 128), F32),
            pltpu.VMEM((PARTS, block, width), BF16),
            pltpu.VMEM((block // 128, block, 128), F32),
            pltpu.VMEM((n_fsdp, lines, block), BF16),
            pltpu.VMEM((n_fsdp, lines, block), BF16),
            pltpu.VMEM((8, 128), jnp.int32),
            pltpu.SMEM((8, 128), jnp.int32),
            pltpu.SemaphoreType.DMA((n_rep,)),
            pltpu.SemaphoreType.DMA,
            pltpu.SemaphoreType.DMA,
            pltpu.SemaphoreType.DMA((2, far, PARTS, n_col // GROUP)),
            pltpu.SemaphoreType.DMA((2, far, PARTS, n_col // GROUP)),
            pltpu.SemaphoreType.DMA((PARTS,)),
            pltpu.SemaphoreType.DMA((PARTS,)),
            pltpu.SemaphoreType.DMA,
            pltpu.SemaphoreType.DMA,
            pltpu.SemaphoreType.REGULAR,
        ],
        compiler_params=pltpu.CompilerParams(
            collective_id=0, has_side_effects=True, vmem_limit_bytes=60 * 1024 * 1024
        ),
        cost_estimate=pl.CostEstimate(
            flops=40 * block**3, bytes_accessed=6 * 1024 * 1024, transcendentals=0
        ),
    )(x, s, owner_table, newton_counts)
    return out.reshape(lines, 1, cols)


def solution(mesh):
    return jax.shard_map(
        body,
        mesh=mesh,
        in_specs=(P("rep", None, "fsdp", None), P("rep", "fsdp", None, None, None, None), P(), P()),
        out_specs=P("rep", "fsdp", None),
        check_vma=False,
    )
```

time: 76.8 us -> 70.9 us (0.923)
  local copies, waits for them, and re-layouts: 5.14 us -> 1.64 us
  Pallas kernels: 71.4 us -> 69.1 us
    unnamed x9 -> x1, local copies, waits for them, and re-layouts: 5.14 us -> 1.64 us
    pallas_call x1, Pallas kernels: 71.4 us -> 69.1 us  [body(): pl.pallas_call(functools.partial(kernel, n_rep, n_fsdp, n_col), out_shape...]
where the time goes in v2:
time: 70.9 us; the launch traced here: 70.7 us
  Pallas kernels  69.1 us (97%)
  local copies, waits for them, and re-layouts  1.64 us (2%)
    pallas_call x1, Pallas kernels, body(): pl.pallas_call(functools.partial(kernel, n_rep, n_fsdp, n_col), out_shape...  69.1 us
    unnamed x1, local copies, waits for them, and re-layouts  1.64 us

profile of v2, /device:TPU:1, one launch (start us, length us, event | category | flops | bytes accessed | tf_op | source)
XLA Modules:
  0.0 70.7 jit_solution(4345835269453478147)
XLA Ops:
  0.0 69.1 %shard_map.46 = bf16[8,14336]{1,0:T(8,128)(2,1)} custom-call(bf16[8,8,14336]{2,1,0:T(8,128)(2,1)} %bitcast.5, f32[2,512,512]{2,1,0:T(8,128)} %bitcast.4, s32[224]{0:T(256)} %owner_ref.1, s32[224]{0:T(256)} %count_ref.1), custom_call_target="tpu_custom_call" | custom-call | flops 5368709120 | bytes 6291456 | tf_op jit(solution)/shard_map/pallas_call | solution.py:309
  69.1 1.6 %copy.6 = bf16[8,1,14336]{2,0,1:T(8,128)(2,1)} copy(bf16[8,1,14336]{2,0,1:T(8,128)(2,1)} %bitcast.3) | data formatting | bytes 458752

commit v3 on v2

--- a/solution.py
+++ b/solution.py
@@ -21,10 +21,10 @@
 
 def kernel(
     n_rep, n_fsdp, n_col,
-    x_hbm, s_hbm, owner_ref, count_ref, out_ref,
-    x_v, s_v, ring_out, ring_in, summed, packed, g_in, g_f, g_n, d_f, d_out, d_in,
-    blk_v, blk_s,
-    x_sem, s_sem, blk_sem, ring_send, ring_recv, fwd_send, fwd_recv, back_send, back_recv, near_sem,
+    x_hbm, s_hbm, owner_hbm, count_hbm, out_ref,
+    x_v, s_v, ring_out, ring_in, summed, packed, g_in, packed0, mid0, g_in0, g_f, g_n, d_f, d_out, d_in,
+    owner_ref, count_ref, blk_v, blk_s,
+    x_sem, s_sem, table_sem, blk_sem, ring_send, ring_recv, fwd_send, fwd_recv, back_send, back_recv, near_sem, mid_send, mid_recv,
 ):
     rep = lax.axis_index("rep")
     me = lax.axis_index("fsdp")
@@ -66,6 +66,12 @@
     order.append(0)
 
     x_copy(far).start()
+    tables = [
+        pltpu.make_async_copy(owner_hbm, owner_ref, table_sem.at[0]),
+        pltpu.make_async_copy(count_hbm, count_ref, table_sem.at[1]),
+    ]
+    for copy in tables:
+        copy.start()
     greet(barrier, rep=up)
     greet(barrier, rep=down)
     lax.fori_loop(1, outer, greet_planes, 0)
@@ -75,6 +81,8 @@
     s_copy = pltpu.make_async_copy(s_hbm, s_v, s_sem)
     s_copy.start()
 
+    for copy in tables:
+        copy.wait()
     lanes = lax.broadcasted_iota(jnp.int32, blk_v.shape, 1)
     slots = jnp.zeros(blk_v.shape, jnp.int32)
     for j in range(n_col):
@@ -133,33 +141,82 @@
                 total = total + ring_in[way, far - 1, p, j].astype(F32)
             summed[p, j] = total.astype(BF16)
 
-    def fwd_copy(w, p):
+    def plane_copy(t):
+        z = lax.rem(plane + t, outer)
         return pltpu.make_async_remote_copy(
-            src_ref=packed.at[p, w],
-            dst_ref=g_in.at[p, me],
-            send_sem=fwd_send.at[p],
-            recv_sem=fwd_recv.at[p],
+            src_ref=packed0.at[z],
+            dst_ref=mid0.at[plane],
+            send_sem=mid_send,
+            recv_sem=mid_recv,
+            device_id={"fsdp": z * INNER + place},
+            device_id_type=pl.DeviceIdType.MESH,
+        )
+
+    def place_copy(t):
+        u = lax.rem(place + t, INNER)
+        return pltpu.make_async_remote_copy(
+            src_ref=mid0.at[:, u],
+            dst_ref=g_in0.at[:, place],
+            send_sem=fwd_send.at[0],
+            recv_sem=fwd_recv.at[0],
+            device_id={"fsdp": plane * INNER + u},
+            device_id_type=pl.DeviceIdType.MESH,
+        )
+
+    def to_planes():
+        def send(t, carry):
+            z = lax.rem(plane + t, outer)
+            for u in range(INNER):
+                packed0[z, u] = summed[0, blk_s[0, z * INNER + u]]
+            plane_copy(t).start()
+            return carry
+
+        lax.fori_loop(1, outer, send, 0)
+        for u in range(INNER):
+            mid0[plane, u] = summed[0, blk_s[0, plane * INNER + u]]
+
+    def to_places():
+        await_bytes(mid_recv, mid0, outer)
+
+        def send(t, carry):
+            place_copy(t).start()
+            return carry
+
+        lax.fori_loop(1, INNER, send, 0)
+        for z in range(outer):
+            g_in0[z, place] = mid0[z, place]
+
+    def fwd_copy(w):
+        return pltpu.make_async_remote_copy(
+            src_ref=packed.at[w],
+            dst_ref=g_in.at[me],
+            send_sem=fwd_send.at[1],
+            recv_sem=fwd_recv.at[1],
             device_id={"fsdp": w},
             device_id_type=pl.DeviceIdType.MESH,
         )
 
-    def forward(p, lo, hi):
+    def forward(lo, hi):
         def send(t, carry):
             w = lax.rem(me + t, n_fsdp)
-            packed[p, w] = summed[p, blk_s[0, w]]
-            fwd_copy(w, p).start()
+            packed[w] = summed[1, blk_s[0, w]]
+            fwd_copy(w).start()
             return carry
 
         lax.fori_loop(lo, hi, send, 0)
 
-    def await_bytes(sem, buffer):
-        part = buffer.at[pl.ds(0, n_fsdp - 1)]
+    def await_bytes(sem, buffer, count):
+        part = buffer.at[pl.ds(0, count - 1)]
         pltpu.make_async_copy(part, part, sem).wait()
 
     def gather(p):
-        g_in[p, me] = summed[p, blk_s[0, me]]
-        await_bytes(fwd_recv.at[p], g_in.at[p])
-        lines = g_in[p].astype(F32).reshape(block, width)
+        if p == 0:
+            await_bytes(fwd_recv.at[0], g_in0, INNER)
+            lines = g_in0[...].astype(F32).reshape(block, width)
+        else:
+            g_in[me] = summed[1, blk_s[0, me]]
+            await_bytes(fwd_recv.at[1], g_in, n_fsdp)
+            lines = g_in[...].astype(F32).reshape(block, width)
         for q in range(width // 128):
             at = p * (width // 128) + q
             g_f[at] = lines[:, q * 128:(q + 1) * 128]
@@ -172,9 +229,10 @@
         for way in range(2):
             for copy in flight[way]:
                 copy.wait_send()
-        for p in range(PARTS):
-            await_bytes(fwd_send.at[p], packed.at[p])
-        await_bytes(back_send, d_out)
+        await_bytes(mid_send, packed0, outer)
+        await_bytes(fwd_send.at[0], mid0, INNER)
+        await_bytes(fwd_send.at[1], packed, n_fsdp)
+        await_bytes(back_send, d_out, n_fsdp)
 
     x_wait(far)
     blk_copy.wait()
@@ -199,15 +257,18 @@
     part0, part1 = steps(0), steps(1)
     run(part0[0])
     lax.fori_loop(1, INNER, greet_near, 0)
-    run(part1[0])
-    for a, b in zip(part0[1:], part1[1:]):
-        run(a)
-        run(b)
+    for stage in (part0[1], part0[2], part1[0], part1[1], part0[3], part1[2], part0[4], part1[3]):
+        run(stage)
+    for g in range(groups):
+        finish(0, g)
+    to_planes()
+    for stage in (part1[4],):
+        run(stage)
     pl.semaphore_wait(near_sem, INNER - 1)
-    for p in range(PARTS):
-        for g in range(groups):
-            finish(p, g)
-        forward(p, 1, n_fsdp)
+    for g in range(groups):
+        finish(1, g)
+    forward(1, n_fsdp)
+    to_places()
     s_copy.wait()
     gather(0)
     left = g_n[0]
@@ -288,7 +349,7 @@
     lax.fori_loop(1, n_fsdp // 2, send_both, 0)
     d_in[me] = lines_of(me)
 
-    await_bytes(back_recv, d_in)
+    await_bytes(back_recv, d_in, n_fsdp)
     for j in range(n_col):
         out_ref[:, j * block:(j + 1) * block] = d_in[owner_ref[rep * n_col + j]]
 
@@ -310,10 +371,10 @@
         functools.partial(kernel, n_rep, n_fsdp, n_col),
         out_shape=jax.ShapeDtypeStruct((lines, cols), BF16),
         in_specs=[
-            pl.BlockSpec(memory_space=pl.ANY),
-            pl.BlockSpec(memory_space=pl.ANY),
-            pl.BlockSpec(memory_space=pltpu.SMEM),
-            pl.BlockSpec(memory_space=pltpu.SMEM),
+            pl.BlockSpec(memory_space=pltpu.HBM),
+            pl.BlockSpec(memory_space=pltpu.HBM),
+            pl.BlockSpec(memory_space=pltpu.HBM),
+            pl.BlockSpec(memory_space=pltpu.HBM),
         ],
         out_specs=pl.BlockSpec(memory_space=pltpu.VMEM),
         scratch_shapes=[
@@ -322,17 +383,23 @@
             pltpu.VMEM((2, far, PARTS, n_col, lines, width), BF16),
             pltpu.VMEM((2, far, PARTS, n_col, lines, width), BF16),
             pltpu.VMEM((PARTS, n_col, lines, width), BF16),
-            pltpu.VMEM((PARTS, n_fsdp, lines, width), BF16),
-            pltpu.VMEM((PARTS, n_fsdp, lines, width), BF16),
+            pltpu.VMEM((n_fsdp, lines, width), BF16),
+            pltpu.VMEM((n_fsdp, lines, width), BF16),
+            pltpu.VMEM((n_fsdp // INNER, INNER, lines, width), BF16),
+            pltpu.VMEM((n_fsdp // INNER, INNER, lines, width), BF16),
+            pltpu.VMEM((n_fsdp // INNER, INNER, lines, width), BF16),
             pltpu.VMEM((block // 128, block, 128), F32),
             pltpu.VMEM((PARTS, block, width), BF16),
             pltpu.VMEM((block // 128, block, 128), F32),
             pltpu.VMEM((n_fsdp, lines, block), BF16),
             pltpu.VMEM((n_fsdp, lines, block), BF16),
+            pltpu.SMEM(owner_table.shape, jnp.int32),
+            pltpu.SMEM(newton_counts.shape, jnp.int32),
             pltpu.VMEM((8, 128), jnp.int32),
             pltpu.SMEM((8, 128), jnp.int32),
             pltpu.SemaphoreType.DMA((n_rep,)),
             pltpu.SemaphoreType.DMA,
+            pltpu.SemaphoreType.DMA((2,)),
             pltpu.SemaphoreType.DMA,
             pltpu.SemaphoreType.DMA((2, far, PARTS, n_col // GROUP)),
             pltpu.SemaphoreType.DMA((2, far, PARTS, n_col // GROUP)),
@@ -341,14 +408,16 @@
             pltpu.SemaphoreType.DMA,
             pltpu.SemaphoreType.DMA,
             pltpu.SemaphoreType.REGULAR,
+            pltpu.SemaphoreType.DMA,
+            pltpu.SemaphoreType.DMA,
         ],
         compiler_params=pltpu.CompilerParams(
-            collective_id=0, has_side_effects=True, vmem_limit_bytes=60 * 1024 * 1024
+            collective_id=0, has_side_effects=True, vmem_limit_bytes=40 * 1024 * 1024
         ),
         cost_estimate=pl.CostEstimate(
             flops=40 * block**3, bytes_accessed=6 * 1024 * 1024, transcendentals=0
         ),
-    )(x, s, owner_table, newton_counts)
+    )(*[pltpu.with_memory_space_constraint(v, pltpu.HBM) for v in (x, s, owner_table, newton_counts)])
     return out.reshape(lines, 1, cols)
 
 

time: 70.9 us -> 68.5 us (0.966)
  Pallas kernels: 69.1 us -> 67.7 us
  local copies, waits for them, and re-layouts: 1.64 us -> 0.69 us
    pallas_call x1, Pallas kernels: 69.1 us -> 67.7 us  [body(): pl.pallas_call(functools.partial(kernel, n_rep, n_fsdp, n_col), out_shape...]
    unnamed x1, local copies, waits for them, and re-layouts: 1.64 us -> 0.69 us
where the time goes in v3:
time: 68.5 us; the launch traced here: 68.4 us
  Pallas kernels  67.7 us (99%)
  local copies, waits for them, and re-layouts  0.69 us (1%)
    pallas_call x1, Pallas kernels, body(): pl.pallas_call(functools.partial(kernel, n_rep, n_fsdp, n_col), out_shape...  67.7 us

profile of v3, /device:TPU:1, one launch (start us, length us, event | category | flops | bytes accessed | tf_op | source)
XLA Modules:
  0.0 68.4 jit_solution(9865511832479086451)
XLA Ops:
  0.0 67.7 %shard_map.46 = bf16[8,14336]{1,0:T(8,128)(2,1)S(1)} custom-call(bf16[8,8,14336]{2,1,0:T(8,128)(2,1)} %bitcast.5, f32[2,512,512]{2,1,0:T(8,128)} %bitcast.4, s32[224]{0:T(256)} %owner_hbm.1, s32[224]{0:T(256)} %count_hbm.1), custom_call_target="tpu_custom_call" | custom-call | flops 5368709120 | bytes 6291456 | tf_op jit(solution)/shard_map/pallas_call | solution.py:370
  67.7 0.7 %copy.6 = bf16[8,1,14336]{2,0,1:T(8,128)(2,1)} copy(bf16[8,1,14336]{2,0,1:T(8,128)(2,1)S(1)} %bitcast.3) | data formatting | bytes 458752

commit v4 on v3

--- a/solution.py
+++ b/solution.py
@@ -11,8 +11,8 @@
 BF16 = jnp.bfloat16
 PARTS = 2
 INNER = 8
-DEPTH = 2
-GROUP = 14
+DEPTH = 4
+GROUP = 7
 
 
 def mm(a, b, dims=((1,), (0,))):
@@ -316,9 +316,9 @@
     halfway = mm(roots[0], grad).astype(BF16)
     precond = mm(halfway, roots[1])
     pre_mass = jnp.sum(precond * precond)
-    scaled = precond * jnp.sqrt(grad_mass / (pre_mass + 1e-6))
+    scale = jnp.sqrt(grad_mass / (pre_mass + 1e-6))
     for q in range(block // 128):
-        d_f[q] = scaled[:, q * 128:(q + 1) * 128]
+        d_f[q] = precond[:, q * 128:(q + 1) * 128]
 
     def back_copy(w):
         return pltpu.make_async_remote_copy(
@@ -331,9 +331,8 @@
         )
 
     def lines_of(w):
-        return jnp.concatenate(
-            [d_f[q, pl.ds(w, thin, stride=n_fsdp), :] for q in range(block // 128)], axis=1
-        ).astype(BF16)
+        lines = [d_f[q, pl.ds(w, thin, stride=n_fsdp), :] for q in range(block // 128)]
+        return (jnp.concatenate(lines, axis=1) * scale).astype(BF16)
 
     def send_back(t, carry):
         w = lax.rem(me + t, n_fsdp)

time: 68.5 us -> 68 us (level)
  no operation moved by 1% of the time
where the time goes in v4:
time: 68 us; the launch traced here: 67.9 us
  Pallas kernels  67.2 us (99%)
  local copies, waits for them, and re-layouts  0.69 us (1%)
    pallas_call x1, Pallas kernels, body(): pl.pallas_call(functools.partial(kernel, n_rep, n_fsdp, n_col), out_shape...  67.2 us

profile of v4, /device:TPU:1, one launch (start us, length us, event | category | flops | bytes accessed | tf_op | source)
XLA Modules:
  0.0 67.9 jit_solution(4259475569531479754)
XLA Ops:
  0.0 67.2 %shard_map.46 = bf16[8,14336]{1,0:T(8,128)(2,1)S(1)} custom-call(bf16[8,8,14336]{2,1,0:T(8,128)(2,1)} %bitcast.5, f32[2,512,512]{2,1,0:T(8,128)} %bitcast.4, s32[224]{0:T(256)} %owner_hbm.1, s32[224]{0:T(256)} %count_hbm.1), custom_call_target="tpu_custom_call" | custom-call | flops 5368709120 | bytes 6291456 | tf_op jit(solution)/shard_map/pallas_call | solution.py:369
  67.2 0.7 %copy.6 = bf16[8,1,14336]{2,0,1:T(8,128)(2,1)} copy(bf16[8,1,14336]{2,0,1:T(8,128)(2,1)S(1)} %bitcast.3) | data formatting | bytes 458752
